TPU v7x, 32 devices: a whole 2x2x4 slice. The times are simulated.
32 devices in a mesh: dp: 8 (over z, x), row: 2 (over y), col: 2 (over core).
Axes of the slice: x: 2, y: 2, z: 4, core: 2. Of those that a mesh axis runs over, the one named last changes fastest.
Arguments:
- inputs: bfloat16 [4096, 2048], P('dp', ('col', 'row')), may hold values from -6 to 6
- norm_gain: bfloat16 [2048], P(('col', 'row')), may hold values from 0.5 to 1.5
- norm_shift: bfloat16 [2048], P(('col', 'row')), may hold values from -3 to 3
- qkv_weight: bfloat16 [2048, 6144], P('col', 'row'), may hold values from -0.125 to 0.125
- qkv_bias: bfloat16 [6144], P(('row', 'col')), may hold values from -3 to 3
- up_weight: bfloat16 [2048, 8192], P('col', 'row')
- up_bias: bfloat16 [8192], P(('row', 'col')), may hold values from -3 to 3
- dense_weight: bfloat16 [2048, 2048], P('row', 'col'), may hold values from -0.75 to 0.75
- down_weight: bfloat16 [8192, 2048], P('row', 'col'), may hold values from -0.0625 to 0.0625
- out_bias: bfloat16 [2048], P(('col', 'row')), may hold values from -3 to 3
- cotangent: bfloat16 [4096, 2048], P('dp', ('col', 'row')), may hold values from -6 to 6
- seq_lengths: int32 [32], replicated, may hold values from 1 to 512, as said below
- seq_owner: int32 [32], replicated, may hold values from 0 to 7, as said below
Outputs:
- outputs: bfloat16 [4096, 2048], P('dp', ('col', 'row'))
- grad_inputs: float32 [4096, 2048], P('dp', ('col', 'row'))
- grad_norm_gain: float32 [2048], P(('col', 'row'))
- grad_norm_shift: float32 [2048], P(('col', 'row'))
- grad_qkv_weight: float32 [2048, 6144], P(('col', 'dp'), 'row')
- grad_qkv_bias: float32 [6144], P(('row', 'col'))
- grad_up_weight: float32 [2048, 8192], P(('col', 'dp'), 'row')
- grad_up_bias: float32 [8192], P(('row', 'col'))
- grad_dense_weight: float32 [2048, 2048], P(('row', 'dp'), 'col')
- grad_down_weight: float32 [8192, 2048], P(('row', 'dp'), 'col')
- grad_out_bias: float32 [2048], P(('col', 'row'))
Inputs may be any that keep to these rules, and one draw needn't show every extreme that they name: `seq_lengths`: the lengths of the sequences held by one index of dp sum to at most 512; in every draw one sequence is 512 long and is the only one of its index. `seq_owner`: loads differ between indices of dp; an index may hold no sequence.
All inputs are finite; a program needn't handle non-finite values.
Results may differ from a plain program's by a relative error of at most 0.0097.
Values may be sent and summed in bfloat16 or wider, within the bound.
A program may use at most 256 MiB of HBM per device.

v0:
```python
from functools import partial

import jax
import jax.numpy as jnp
from jax import lax
from jax.sharding import PartitionSpec as P

D = 2048
HEAD_DIM = 64
ROT = 32


epsilon = 1e-05
masked_score = -1e30
rope_base = 10000.0


def layout(seq_lengths, seq_owner, device, row_count):
    owned = seq_owner == device
    lengths_owned = jnp.where(owned, seq_lengths, 0)
    seq_ends = jnp.cumsum(lengths_owned, dtype=jnp.int32)
    seq_starts = seq_ends - lengths_owned
    slot_index = jnp.arange(row_count, dtype=jnp.int32)
    segment = jnp.sum((seq_ends[None, :] <= slot_index[:, None]).astype(jnp.int32), axis=1)
    picked = jnp.arange(seq_lengths.shape[0], dtype=jnp.int32)[None, :] == segment[:, None]
    seq_begin = jnp.sum(jnp.where(picked, seq_starts[None, :], 0), axis=1)
    position = slot_index - seq_begin
    is_valid = slot_index < seq_ends[-1]
    return (segment, position, is_valid)


def angles(position):
    index_range = jnp.arange(ROT // 2, dtype=jnp.float32)
    frequency = rope_base ** (-2.0 * index_range / ROT)
    phase = position.astype(jnp.float32)[:, None] * frequency[None, :]
    return (jnp.cos(phase)[:, None, :], jnp.sin(phase)[:, None, :])


def rotate(field, cosines, sines):
    half_rot = cosines.shape[-1]
    first_part = field[..., :half_rot]
    second_part = field[..., half_rot : 2 * half_rot]
    return jnp.concatenate(
        [
            first_part * cosines - second_part * sines,
            second_part * cosines + first_part * sines,
            field[..., 2 * half_rot :],
        ],
        axis=-1,
    )


def contract_rows(left, right):
    return lax.dot_general(
        left, right, (((0,), (0,)), ((), ())), preferred_element_type=jnp.float32
    )


def contract_cols(left, right):
    return lax.dot_general(
        left, right, (((1,), (1,)), ((), ())), preferred_element_type=jnp.float32
    )


def on_device(
    inputs,
    norm_gain,
    norm_shift,
    qkv_weight,
    qkv_bias,
    up_weight,
    up_bias,
    dense_weight,
    down_weight,
    out_bias,
    cotangent,
    seq_lengths,
    seq_owner,
):
    row_count = inputs.shape[0]
    device = lax.axis_index("dp")
    segment, position, is_valid = layout(seq_lengths, seq_owner, device, row_count)
    valid_col = is_valid.astype(jnp.float32)[:, None]
    source = inputs.astype(jnp.float32)
    total_one, total_two = lax.psum(
        (jnp.sum(source, axis=1), jnp.sum(source * source, axis=1)), ("row", "col")
    )
    average = total_one / D
    variance = total_two / D - average * average
    scale_inv = lax.rsqrt(variance + epsilon)[:, None]
    normed = (source - average[:, None]) * scale_inv
    gain_values = norm_gain.astype(jnp.float32)
    hidden = (normed * gain_values + norm_shift.astype(jnp.float32)).astype(jnp.bfloat16)
    hidden_rows = lax.all_gather(hidden, "row", axis=1, tiled=True)
    projected_part = jnp.dot(hidden_rows, qkv_weight, preferred_element_type=jnp.float32)
    before_part = jnp.dot(hidden_rows, up_weight, preferred_element_type=jnp.float32)
    projected, before = (
        lax.psum_scatter(projected_part, "col", scatter_dimension=1, tiled=True),
        lax.psum_scatter(before_part, "col", scatter_dimension=1, tiled=True),
    )
    projected = projected + qkv_bias.astype(jnp.float32)
    before = before + up_bias.astype(jnp.float32)
    activated = jax.nn.gelu(before, approximate=True).astype(jnp.bfloat16)
    head_count = projected.shape[1] // (3 * HEAD_DIM)
    grouped = projected.reshape(row_count, head_count, 3, HEAD_DIM)
    cosines, sines = angles(position)
    queries = rotate(grouped[:, :, 0], cosines, sines).astype(jnp.bfloat16)
    key_rows = rotate(grouped[:, :, 1], cosines, sines).astype(jnp.bfloat16)
    values = grouped[:, :, 2].astype(jnp.bfloat16)
    block_rows = min(512, row_count)
    score_scale = HEAD_DIM ** (-0.5)
    slot_index = jnp.arange(row_count, dtype=jnp.int32)

    def block_scores(first_row, last_key):
        scores = (
            jnp.einsum("qhd,khd->hqk", queries, key_rows, preferred_element_type=jnp.float32)
            * score_scale
        )
        allowed = (segment[first_row:last_key, None] == segment[None, :last_key]) & (
            slot_index[None, :last_key] <= slot_index[first_row:last_key, None]
        )
        return jnp.where(allowed[None], scores, masked_score)

    number = 0
    first_row = number * block_rows
    last_key = first_row + block_rows
    scores = block_scores(first_row, last_key)
    row_max = jnp.max(scores, axis=-1, keepdims=True)
    weights = jnp.exp(scores - row_max)
    row_total = jnp.sum(weights, axis=-1, keepdims=True)
    probabilities = weights / row_total
    log_totals = [row_max + jnp.log(row_total)]
    pieces = jnp.einsum(
        "hqk,khd->qhd",
        probabilities.astype(jnp.bfloat16),
        values,
        preferred_element_type=jnp.float32,
    )
    attended = pieces.reshape(row_count, head_count * HEAD_DIM).astype(jnp.bfloat16)
    attended_rows, activated_rows = (
        lax.all_gather(attended, "col", axis=1, tiled=True),
        lax.all_gather(activated, "col", axis=1, tiled=True),
    )
    branch_part = jnp.dot(
        attended_rows, dense_weight, preferred_element_type=jnp.float32
    ) + jnp.dot(activated_rows, down_weight, preferred_element_type=jnp.float32)
    branch = lax.psum_scatter(branch_part, "row", scatter_dimension=1, tiled=True)
    outputs = (source + valid_col * (branch + out_bias.astype(jnp.float32))).astype(jnp.bfloat16)
    grad_branch = cotangent * is_valid.astype(jnp.bfloat16)[:, None]
    branch_rows = lax.all_gather(grad_branch, "row", axis=1, tiled=True)
    grad_dense = contract_rows(attended_rows, branch_rows)
    grad_down = contract_rows(activated_rows, branch_rows)
    grad_bias_out = jnp.sum(grad_branch.astype(jnp.float32), axis=0)
    grad_dense, grad_down = (
        lax.psum_scatter(grad_dense, "dp", scatter_dimension=0, tiled=True),
        lax.psum_scatter(grad_down, "dp", scatter_dimension=0, tiled=True),
    )
    attended_part = contract_cols(branch_rows, dense_weight)
    activated_part = contract_cols(branch_rows, down_weight)
    d_attended, d_activated = (
        lax.psum_scatter(attended_part, "col", scatter_dimension=1, tiled=True),
        lax.psum_scatter(activated_part, "col", scatter_dimension=1, tiled=True),
    )
    unused_value, gelu_back = jax.vjp(partial(jax.nn.gelu, approximate=True), before)
    d_before = gelu_back(d_activated)[0].astype(jnp.bfloat16)
    grad_up_bias = jnp.sum(d_before.astype(jnp.float32), axis=0)
    d_mixed = d_attended.astype(jnp.bfloat16).reshape(row_count, head_count, HEAD_DIM)
    key_grads = jnp.zeros((row_count, head_count, HEAD_DIM), jnp.float32)
    value_grads = jnp.zeros((row_count, head_count, HEAD_DIM), jnp.float32)
    number = 0
    first_row = number * block_rows
    last_key = first_row + block_rows
    scores = block_scores(first_row, last_key)
    probabilities = jnp.exp(scores - log_totals[number])
    d_probs = jnp.einsum("qhd,khd->hqk", d_mixed, values, preferred_element_type=jnp.float32)
    row_dot = jnp.sum(probabilities * d_probs, axis=-1, keepdims=True)
    d_scores = (probabilities * (d_probs - row_dot)).astype(jnp.bfloat16)
    query_grads = (
        jnp.einsum("hqk,khd->qhd", d_scores, key_rows, preferred_element_type=jnp.float32)
        * score_scale
    )
    key_grads = key_grads.at[:last_key].add(
        jnp.einsum("hqk,qhd->khd", d_scores, queries, preferred_element_type=jnp.float32)
        * score_scale
    )
    value_grads = value_grads.at[:last_key].add(
        jnp.einsum(
            "hqk,qhd->khd",
            probabilities.astype(jnp.bfloat16),
            d_mixed,
            preferred_element_type=jnp.float32,
        )
    )
    d_queries = rotate(query_grads, cosines, -sines)
    d_keys = rotate(key_grads, cosines, -sines)
    d_projected = (
        jnp.stack([d_queries, d_keys, value_grads], axis=2)
        .reshape(row_count, 3 * head_count * HEAD_DIM)
        .astype(jnp.bfloat16)
    )
    grad_qkv_bias = jnp.sum(d_projected.astype(jnp.float32), axis=0)
    projected_rows, before_rows = (
        lax.all_gather(d_projected, "col", axis=1, tiled=True),
        lax.all_gather(d_before, "col", axis=1, tiled=True),
    )
    grad_qkv = contract_rows(hidden_rows, projected_rows)
    grad_up = contract_rows(hidden_rows, before_rows)
    hidden_part = contract_cols(projected_rows, qkv_weight) + contract_cols(before_rows, up_weight)
    d_hidden = lax.psum_scatter(hidden_part, "row", scatter_dimension=1, tiled=True)
    grad_gain = jnp.sum(d_hidden * normed, axis=0)
    grad_shift = jnp.sum(d_hidden, axis=0)
    d_normed = d_hidden * gain_values
    part_one, part_two = lax.psum(
        (jnp.sum(d_normed, axis=1), jnp.sum(d_normed * normed, axis=1)), ("row", "col")
    )
    grad_inputs = cotangent.astype(jnp.float32) + scale_inv * (
        d_normed - part_one[:, None] / D - normed * part_two[:, None] / D
    )
    grad_qkv, grad_up = (
        lax.psum_scatter(grad_qkv, "dp", scatter_dimension=0, tiled=True),
        lax.psum_scatter(grad_up, "dp", scatter_dimension=0, tiled=True),
    )
    grad_gain, grad_shift, grad_qkv_bias, grad_up_bias, grad_bias_out = lax.psum(
        (grad_gain, grad_shift, grad_qkv_bias, grad_up_bias, grad_bias_out), "dp"
    )
    return (
        outputs,
        grad_inputs,
        grad_gain,
        grad_shift,
        grad_qkv,
        grad_qkv_bias,
        grad_up,
        grad_up_bias,
        grad_dense,
        grad_down,
        grad_bias_out,
    )


def solution(mesh):
    in_specs = (
        P("dp", ("col", "row")),
        P(("col", "row")),
        P(("col", "row")),
        P("col", "row"),
        P(("row", "col")),
        P("col", "row"),
        P(("row", "col")),
        P("row", "col"),
        P("row", "col"),
        P(("col", "row")),
        P("dp", ("col", "row")),
        P(),
        P(),
    )
    out_specs = (
        P("dp", ("col", "row")),
        P("dp", ("col", "row")),
        P(("col", "row")),
        P(("col", "row")),
        P(("col", "dp"), "row"),
        P(("row", "col")),
        P(("col", "dp"), "row"),
        P(("row", "col")),
        P(("row", "dp"), "col"),
        P(("row", "dp"), "col"),
        P(("col", "row")),
    )
    return jax.shard_map(
        on_device, mesh=mesh, in_specs=in_specs, out_specs=out_specs, check_vma=False
    )
```

profile of v0, /device:TPU:9, one launch (start us, length us, event | category | flops | bytes accessed | tf_op | source)
XLA Modules:
  0.0 1147.2 jit_solution(15883329504396813821)
XLA Ops:
  14.7 5.7 all-reduce.2
  22.7 12.0 %all-gather.13.cloned.1.call-done = bf16[512,1024]{1,0:T(8,128)(2,1)} async-done(((bf16[512,512]{1,0:T(8,128)(2,1)}), bf16[512,1024]{1,0:T(8,128)(2,1)}) %all-gather.13.cloned.1.call-update) | async-done | bytes 1048592 | tf_op jit(solution)/shard_map/all_gather | solution.py:150
  38.6 19.5 %all-gather.7.cloned.1.call-done = bf16[512,1024]{1,0:T(8,128)(2,1)} async-done(((bf16[512,512]{1,0:T(8,128)(2,1)}), bf16[512,1024]{1,0:T(8,128)(2,1)}) %all-gather.7.cloned.1.call-update) | async-done | bytes 1048592 | tf_op jit(solution)/shard_map/all_gather | solution.py:94
  58.1 9.2 fusion.50
  68.6 10.5 fusion.54
  80.3 11.0 fusion.51
  109.4 20.4 %reduce-scatter.13.cloned.1.call-done = f32[512,2048]{1,0:T(8,128)} async-done(((f32[512,4096]{1,0:T(8,128)}), f32[512,2048]{1,0:T(8,128)}) %reduce-scatter.13.cloned.1.call-update) | async-done | bytes 4194320 | tf_op jit(solution)/shard_map/reduce_scatter | solution.py:99
  129.8 7.4 convert_reduce_fusion
  153.6 6.0 fusion.18
  159.7 11.6 %fusion.55 = f32[512,1024]{1,0:T(8,128)} fusion(bf16[512,4096]{1,0:T(8,128)(2,1)} %all-gather.17.cloned.1.call-done, bf16[1024,4096]{1,0:T(8,128)(2,1)} %param.26), kind=kOutput, calls=%fused_computation.105 | convolution fusion | flops 4294967296 | bytes 14680064 | tf_op jit(solution)/shard_map/dot_general | solution.py:60
  171.3 9.1 convolution_add_fusion
  180.7 4.0 all-gather.11.cloned.1.call-done
  184.8 10.5 fusion.52
  197.0 4.5 convolution_add_fusion.1
  201.6 4.5 fusion.58
  207.6 8.3 fusion.56
  215.9 10.4 fusion.57
  227.6 10.3 fusion.59
  241.3 27.7 %all-reduce = (f32[512]{0:T(512)}, f32[512]{0:T(512)}, f32[1536]{0:T(1024)}, f32[2048]{0:T(1024)}, f32[512]{0:T(512)}) all-reduce(f32[512]{0:T(512)S(1)} %get-tuple-element.51, f32[512]{0:T(512)S(1)} %get-tuple-element.54, f32[1536]{0:T(1024)S(1)} %reduce_sum.130, ...), channel_id=1, replica_groups=mesh['dp'=8,'row'=2,'col'=2] {'dp'}, use_global_device_ids=true, to_apply=%region_21.22 | all-reduce | flops 5120 | bytes 40960 | tf_op jit(solution)/shard_map/psum | solution.py:223
  269.0 12.3 %all-reduce.1 = (f32[512]{0:T(512)S(1)}, f32[512]{0:T(512)S(1)}) all-reduce(f32[512]{0:T(512)S(1)} %get-tuple-element.52, f32[512]{0:T(512)S(1)} %get-tuple-element.53), channel_id=1, replica_groups=mesh['dp'=8,'row'=2,'col'=2] {'row','col'}, use_global_device_ids=true, to_apply=%region_19.20 | all-reduce | flops 1024 | bytes 8192 | tf_op jit(solution)/shard_map/psum | solution.py:213
  284.6 73.2 %reduce-scatter.27.cloned.1.call-done = f32[128,1024]{1,0:T(8,128)} async-done(((f32[1024,1024]{1,0:T(8,128)}), f32[128,1024]{1,0:T(8,128)}) %reduce-scatter.27.cloned.1.call-update) | async-done | bytes 524304 | tf_op jit(solution)/shard_map/reduce_scatter | solution.py:155
  357.8 209.6 %reduce-scatter.23.cloned.1.call-done = f32[128,3072]{1,0:T(8,128)} async-done(((f32[1024,3072]{1,0:T(8,128)}), f32[128,3072]{1,0:T(8,128)}) %reduce-scatter.23.cloned.1.call-update) | async-done | bytes 1572880 | tf_op jit(solution)/shard_map/reduce_scatter | solution.py:220
  567.4 286.8 %reduce-scatter.25.cloned.1.call-done = f32[128,4096]{1,0:T(8,128)} async-done(((f32[1024,4096]{1,0:T(8,128)}), f32[128,4096]{1,0:T(8,128)}) %reduce-scatter.25.cloned.1.call-update) | async-done | bytes 2097168 | tf_op jit(solution)/shard_map/reduce_scatter | solution.py:221
  854.2 286.0 %reduce-scatter.29.cloned.1.call-done = f32[512,1024]{1,0:T(8,128)} async-done(((f32[4096,1024]{1,0:T(8,128)}), f32[512,1024]{1,0:T(8,128)}) %reduce-scatter.29.cloned.1.call-update) | async-done | bytes 2097168 | tf_op jit(solution)/shard_map/reduce_scatter | solution.py:156
  (151 shorter events, 61.7 us)
Async XLA Ops:
  7.2 27.5 %copy-start = (bf16[1024,1024]{1,0:T(8,128)(2,1)S(1)}, bf16[1024,1024]{1,0:T(8,128)(2,1)}, u32[]{:S(2)}) copy-start(bf16[1024,1024]{1,0:T(8,128)(2,1)} %param.28) | copy-start | bytes 6291460
  7.2 27.5 %all-gather.13.cloned.1.call-start = ((), (), s32[]{:S(2)}) async-start(), calls=%async_computation.16 | async-start | bytes 1572864 | tf_op jit(solution)/shard_map/all_gather | solution.py:150
  12.0 46.1 %all-gather.7.cloned.1.call-start = ((), (), s32[]{:S(2)}) async-start(), calls=%async_computation.10 | async-start | bytes 1572864 | tf_op jit(solution)/shard_map/all_gather | solution.py:94
  12.8 25.7 %copy-start.13 = (f32[512]{0:T(512)}, f32[512]{0:T(512)S(1)}, u32[]{:S(2)}) copy-start(f32[512]{0:T(512)S(1)} %convert_element_type.103) | copy-start | bytes 6148
  20.4 18.1 %copy-start.15 = (f32[512]{0:T(512)}, f32[512]{0:T(512)S(1)}, u32[]{:S(2)}) copy-start(f32[512]{0:T(512)S(1)} %get-tuple-element.92) | copy-start | bytes 6148
  20.4 18.1 %copy-start.17 = (f32[512]{0:T(512)}, f32[512]{0:T(512)S(1)}, u32[]{:S(2)}) copy-start(f32[512]{0:T(512)S(1)} %get-tuple-element.93) | copy-start | bytes 6148
  22.6 71.4 %reduce-scatter.17.cloned.1.call-start = ((), (), s32[]{:S(2)}) async-start(), calls=%async_computation.17 | async-start | bytes 3145728 | tf_op jit(solution)/shard_map/reduce_scatter | solution.py:161
  38.5 57.1 %reduce-scatter.11.cloned.1.call-start = ((), (), s32[]{:S(2)}) async-start(), calls=%async_computation.11 | async-start | bytes 9437184 | tf_op jit(solution)/shard_map/reduce_scatter | solution.py:98
  67.3 42.1 %reduce-scatter.19.cloned.1.call-start = ((), (), s32[]{:S(2)}) async-start(), calls=%async_computation.19 | async-start | bytes 12582912 | tf_op jit(solution)/shard_map/reduce_scatter | solution.py:162
  79.1 50.6 %reduce-scatter.13.cloned.1.call-start = ((), (), s32[]{:S(2)}) async-start(), calls=%async_computation.13 | async-start | bytes 12582912 | tf_op jit(solution)/shard_map/reduce_scatter | solution.py:99
  91.4 68.3 %all-gather.17.cloned.1.call-start = ((), (), s32[]{:S(2)}) async-start(), calls=%async_computation.20 | async-start | bytes 6291456 | tf_op jit(solution)/shard_map/all_gather | solution.py:204
  137.2 34.1 %all-gather.15.cloned.1.call-start = ((), (), s32[]{:S(2)}) async-start(), calls=%async_computation.18 | async-start | bytes 4718592 | tf_op jit(solution)/shard_map/all_gather | solution.py:203
  139.8 9.7 copy-start.1
  152.6 32.2 %all-gather.11.cloned.1.call-start = ((), (), s32[]{:S(2)}) async-start(), calls=%async_computation.14 | async-start | bytes 6291456 | tf_op jit(solution)/shard_map/all_gather | solution.py:142
  153.3 43.6 %all-gather.9.cloned.1.call-start = ((), (), s32[]{:S(2)}) async-start(), calls=%async_computation.12 | async-start | bytes 1572864 | tf_op jit(solution)/shard_map/all_gather | solution.py:141
  159.6 79.7 %reduce-scatter.21.cloned.1.call-start = ((), (), s32[]{:S(2)}) async-start(), calls=%async_computation.21 | async-start | bytes 3145728 | tf_op jit(solution)/shard_map/reduce_scatter | solution.py:209
  180.4 100.9 %reduce-scatter.15.cloned.1.call-start = ((), (), s32[]{:S(2)}) async-start(), calls=%async_computation.15 | async-start | bytes 3145728 | tf_op jit(solution)/shard_map/reduce_scatter | solution.py:147
  195.2 6.3 copy-start.27
  201.5 156.3 %reduce-scatter.27.cloned.1.call-start = ((), (), s32[]{:S(2)}) async-start(), calls=%async_computation.24 | async-start | bytes 4718592 | tf_op jit(solution)/shard_map/reduce_scatter | solution.py:155
  206.1 361.3 %reduce-scatter.23.cloned.1.call-start = ((), (), s32[]{:S(2)}) async-start(), calls=%async_computation.22 | async-start | bytes 14155776 | tf_op jit(solution)/shard_map/reduce_scatter | solution.py:220
  215.9 638.3 %reduce-scatter.25.cloned.1.call-start = ((), (), s32[]{:S(2)}) async-start(), calls=%async_computation.23 | async-start | bytes 18874368 | tf_op jit(solution)/shard_map/reduce_scatter | solution.py:221
  226.4 913.8 %reduce-scatter.29.cloned.1.call-start = ((), (), s32[]{:S(2)}) async-start(), calls=%async_computation.25 | async-start | bytes 18874368 | tf_op jit(solution)/shard_map/reduce_scatter | solution.py:156
  237.9 3.4 copy-start.19
  238.0 43.4 %copy-start.3 = (bf16[512,512]{1,0:T(8,128)(2,1)S(1)}, bf16[512,512]{1,0:T(8,128)(2,1)}, u32[]{:S(2)}) copy-start(bf16[512,512]{1,0:T(8,128)(2,1)} %param.31) | copy-start | bytes 1572868
  (21 other events, 34.4 us)
Sparse Core Ops, SparseCore 0:
  12.2 22.4 all-gather.12
  36.8 21.2 all-gather.6
  60.9 10.3 reduce-scatter.16
  73.6 15.6 reduce-scatter.10
  91.4 17.9 reduce-scatter.18
  111.7 18.0 reduce-scatter.12
  137.3 14.9 all-gather.16
  154.4 13.2 all-gather.14
  169.9 14.8 all-gather.10
  186.7 10.1 all-gather.8
  199.2 32.2 reduce-scatter.20
  233.7 31.8 reduce-scatter.14
  269.8 87.9 reduce-scatter.26
  362.2 205.1 reduce-scatter.22
  572.1 282.1 reduce-scatter.24
  858.4 281.7 reduce-scatter.28
where the time goes:
time: 1160 us; the launch traced here: 1150 us
  waiting for transfers between devices  917 us (79%)
  matrix products  119 us (10%)
  blocking collectives  45.7 us (4%)
  other arithmetic  34.5 us (3%)
  between operations  14.9 us (1%)
  local copies, waits for them, and re-layouts  14.4 us (1%)
    reduce_scatter x1, waiting for transfers between devices, on_device(): lax.psum_scatter(grad_up, 'dp', scatter_dimension=0, tiled=True)  287 us
    reduce_scatter x1, waiting for transfers between devices, on_device(): lax.psum_scatter(grad_down, 'dp', scatter_dimension=0, tiled=True)  286 us
    reduce_scatter x1, waiting for transfers between devices, on_device(): lax.psum_scatter(grad_qkv, 'dp', scatter_dimension=0, tiled=True)  210 us
    reduce_scatter x1, waiting for transfers between devices, on_device(): lax.psum_scatter(grad_dense, 'dp', scatter_dimension=0, tiled=True)  73.2 us
    dot_general x4, matrix products, contract_cols(): lax.dot_general(left, right, (((1,), (1,)), ((), ())), preferred_element_...  35 us
    dot_general x4, matrix products, contract_rows(): lax.dot_general(left, right, (((0,), (0,)), ((), ())), preferred_element_...  33.6 us
    psum x1, blocking collectives, on_device(): lax.psum((grad_gain, grad_shift, grad_qkv_bias, grad_up_bias, grad_bias_o...  27.7 us
  transfers between devices with their start and end apart: 16, of which 10 were waited for; matrix products, arithmetic and copies ran while one was open for 13% of the time, Pallas kernels for 0%

commit v1 on v0

v1 whole, which is shorter than its diff:
```python
from functools import partial

import jax
import jax.numpy as jnp
from jax import lax
from jax.experimental import pallas as pl
from jax.experimental.pallas import tpu as pltpu
from jax.sharding import PartitionSpec as P

HEAD_DIM = 64
ROT = 32
HALF_ROT = ROT // 2
PAIR = 2 * HEAD_DIM
PAIR_QKV = 3 * PAIR

epsilon = 1e-05
masked_score = -1e30
rope_base = 10000.0
score_scale = HEAD_DIM ** (-0.5)
bf16 = jnp.bfloat16
f32 = jnp.float32


def layout(seq_lengths, seq_owner, device, row_count):
    owned = seq_owner == device
    lengths_owned = jnp.where(owned, seq_lengths, 0)
    seq_ends = jnp.cumsum(lengths_owned, dtype=jnp.int32)
    seq_starts = seq_ends - lengths_owned
    slot_index = jnp.arange(row_count, dtype=jnp.int32)
    segment = jnp.sum((seq_ends[None, :] <= slot_index[:, None]).astype(jnp.int32), axis=1)
    picked = jnp.arange(seq_lengths.shape[0], dtype=jnp.int32)[None, :] == segment[:, None]
    seq_begin = jnp.sum(jnp.where(picked, seq_starts[None, :], 0), axis=1)
    position = slot_index - seq_begin
    is_valid = slot_index < seq_ends[-1]
    return (segment, position, is_valid)


def rotation_tables(position):
    index_range = jnp.arange(HALF_ROT, dtype=f32)
    frequency = rope_base ** (-2.0 * index_range / ROT)
    phase = position.astype(f32)[:, None] * frequency[None, :]
    cosines, sines = jnp.cos(phase), jnp.sin(phase)
    rows = position.shape[0]
    ones = jnp.ones((rows, HEAD_DIM - ROT), f32)
    none = jnp.zeros((rows, HALF_ROT), f32)
    rest = jnp.zeros((rows, HEAD_DIM - ROT), f32)
    same = jnp.concatenate([cosines, cosines, ones], axis=1)
    from_right = jnp.concatenate([sines, none, rest], axis=1)
    from_left = jnp.concatenate([none, sines, rest], axis=1)
    return jnp.stack([same, from_right, from_left])


def attention_kernel(proj_ref, mixed_ref, tables_ref, seg_col_ref, seg_row_ref, attended_ref, grad_ref):
    rows = proj_ref.shape[0]
    block = min(256, rows)
    same, from_right, from_left = tables_ref[0], tables_ref[1], tables_ref[2]

    def rotate(part, sign):
        right = jnp.concatenate([part[:, HALF_ROT:], part[:, :HALF_ROT]], axis=1)
        left = jnp.concatenate([part[:, HEAD_DIM - HALF_ROT :], part[:, : HEAD_DIM - HALF_ROT]], axis=1)
        return part * same - sign * (right * from_right) + sign * (left * from_left)

    def dot(left, right, dims):
        return lax.dot_general(left, right, (dims, ((), ())), preferred_element_type=f32)

    attended_heads, grads = [], []
    for head in range(2):
        base = head * 3 * HEAD_DIM
        queries = rotate(proj_ref[:, base : base + HEAD_DIM], 1.0).astype(bf16)
        keys = rotate(proj_ref[:, base + HEAD_DIM : base + 2 * HEAD_DIM], 1.0).astype(bf16)
        values = proj_ref[:, base + 2 * HEAD_DIM : base + 3 * HEAD_DIM].astype(bf16)
        mixed = mixed_ref[:, head * HEAD_DIM : (head + 1) * HEAD_DIM]
        outs, d_queries, d_keys, d_values = [], [], None, None
        for first in range(0, rows, block):
            last = first + block
            q, d_out = queries[first:last], mixed[first:last]
            k, v = keys[:last], values[:last]
            row_index = first + lax.broadcasted_iota(jnp.int32, (block, last), 0)
            key_index = lax.broadcasted_iota(jnp.int32, (block, last), 1)
            allowed = (seg_col_ref[first:last, :] == seg_row_ref[:, :last]) & (key_index <= row_index)
            scores = jnp.where(allowed, dot(q, k, ((1,), (1,))) * score_scale, masked_score)
            weights = jnp.exp(scores - jnp.max(scores, axis=1, keepdims=True))
            probs = weights * (1.0 / jnp.sum(weights, axis=1, keepdims=True))
            probs_low = probs.astype(bf16)
            outs.append(dot(probs_low, v, ((1,), (0,))))
            d_probs = dot(d_out, v, ((1,), (1,)))
            row_dot = jnp.sum(probs * d_probs, axis=1, keepdims=True)
            d_scores = (probs * (d_probs - row_dot)).astype(bf16)
            d_queries.append(dot(d_scores, k, ((1,), (0,))))
            key_part = dot(d_scores, q, ((0,), (0,)))
            value_part = dot(probs_low, d_out, ((0,), (0,)))
            if d_keys is None:
                d_keys, d_values = key_part, value_part
            else:
                d_keys = jnp.concatenate([key_part[:first] + d_keys, key_part[first:]], axis=0)
                d_values = jnp.concatenate([value_part[:first] + d_values, value_part[first:]], axis=0)
        attended_heads.append(jnp.concatenate(outs, axis=0))
        grads.append(rotate(jnp.concatenate(d_queries, axis=0) * score_scale, -1.0))
        grads.append(rotate(d_keys * score_scale, -1.0))
        grads.append(d_values)
    attended_ref[...] = jnp.concatenate(attended_heads, axis=1).astype(bf16)
    grad_ref[...] = jnp.concatenate(grads, axis=1).astype(bf16)


def attention(projected, mixed, tables, segment):
    rows, width = projected.shape
    pairs = width // PAIR_QKV
    return pl.pallas_call(
        attention_kernel,
        grid=(pairs,),
        in_specs=[
            pl.BlockSpec((rows, PAIR_QKV), lambda i: (0, i)),
            pl.BlockSpec((rows, PAIR), lambda i: (0, i)),
            pl.BlockSpec((3, rows, HEAD_DIM), lambda i: (0, 0, 0)),
            pl.BlockSpec((rows, 1), lambda i: (0, 0)),
            pl.BlockSpec((1, rows), lambda i: (0, 0)),
        ],
        out_specs=[
            pl.BlockSpec((rows, PAIR), lambda i: (0, i)),
            pl.BlockSpec((rows, PAIR_QKV), lambda i: (0, i)),
        ],
        out_shape=[
            jax.ShapeDtypeStruct((rows, pairs * PAIR), bf16),
            jax.ShapeDtypeStruct((rows, width), bf16),
        ],
        compiler_params=pltpu.CompilerParams(vmem_limit_bytes=48 * 1024 * 1024),
        cost_estimate=pl.CostEstimate(
            flops=14 * 2 * pairs * rows * rows * HEAD_DIM * 2,
            bytes_accessed=rows * width * 7,
            transcendentals=2 * pairs * rows * rows,
        ),
        name="attention",
    )(projected, mixed, tables, segment[:, None], segment[None, :])


def dot_plain(left, right):
    return jnp.dot(left, right, preferred_element_type=f32)


def contract_rows(left, right):
    return lax.dot_general(left, right, (((0,), (0,)), ((), ())), preferred_element_type=f32)


def contract_cols(left, right):
    return lax.dot_general(left, right, (((1,), (1,)), ((), ())), preferred_element_type=f32)


def on_device(
    dp_size,
    inputs,
    norm_gain,
    norm_shift,
    qkv_weight,
    qkv_bias,
    up_weight,
    up_bias,
    dense_weight,
    down_weight,
    out_bias,
    cotangent,
    seq_lengths,
    seq_owner,
):
    row_count = inputs.shape[0]
    line = dp_size // 2
    device = lax.axis_index("dp")
    place = device // 2
    side = device % 2
    row = lax.axis_index("row")
    col = lax.axis_index("col")

    over_row = partial(lax.ppermute, axis_name="row", perm=[(0, 1), (1, 0)])
    over_col = partial(lax.ppermute, axis_name="col", perm=[(0, 1), (1, 0)])
    over_side = partial(lax.ppermute, axis_name="dp", perm=[(e, e ^ 1) for e in range(dp_size)])

    def in_order(index, mine, other, axis):
        first = jnp.where(index == 0, mine, other)
        second = jnp.where(index == 0, other, mine)
        return jnp.concatenate([first, second], axis=axis)

    def half_at(array, index, axis):
        width = array.shape[axis] // 2
        return lax.dynamic_slice_in_dim(array, index * width, width, axis)

    segment, position, is_valid = layout(seq_lengths, seq_owner, device, row_count)
    tables = rotation_tables(position)

    gains = jnp.stack([norm_gain, norm_shift])
    grad_branch = cotangent * is_valid.astype(bf16)[:, None]
    inputs_half = in_order(row, inputs, over_row(inputs), 1)
    gains_half = in_order(row, gains, over_row(gains), 1)
    inputs_other = over_col(inputs_half)
    gains_other = over_col(gains_half)
    branch_half = in_order(row, grad_branch, over_row(grad_branch), 1)
    branch_other = over_col(branch_half)

    up_mine, up_other = half_at(up_weight, col, 1), over_col(half_at(up_weight, 1 - col, 1))
    down_mine, down_other = half_at(down_weight, col, 0), over_col(half_at(down_weight, 1 - col, 0))
    qkv_mine, qkv_other = half_at(qkv_weight, col, 1), over_col(half_at(qkv_weight, 1 - col, 1))
    dense_mine, dense_other = half_at(dense_weight, col, 0), over_col(half_at(dense_weight, 1 - col, 0))

    width = 4 * inputs.shape[1]
    source, source_other = inputs_half.astype(f32), inputs_other.astype(f32)
    average = (jnp.sum(source, axis=1) + jnp.sum(source_other, axis=1)) / width
    square = (jnp.sum(source * source, axis=1) + jnp.sum(source_other * source_other, axis=1)) / width
    scale_inv = lax.rsqrt(square - average * average + epsilon)[:, None]

    def hidden_of(rows_in, gain_pair):
        normed = (rows_in - average[:, None]) * scale_inv
        pair = gain_pair.astype(f32)
        return (normed * pair[0] + pair[1]).astype(bf16)

    hidden, hidden_other = hidden_of(source, gains_half), hidden_of(source_other, gains_other)

    before = dot_plain(hidden, up_mine) + dot_plain(hidden_other, up_other) + up_bias.astype(f32)
    activated = jax.nn.gelu(before, approximate=True).astype(bf16)
    d_activated = contract_cols(branch_half, down_mine) + contract_cols(branch_other, down_other)
    unused_value, gelu_back = jax.vjp(partial(jax.nn.gelu, approximate=True), before)
    d_before = gelu_back(d_activated)[0].astype(bf16)

    projected = dot_plain(hidden, qkv_mine) + dot_plain(hidden_other, qkv_other) + qkv_bias.astype(f32)
    d_mixed = (contract_cols(branch_half, dense_mine) + contract_cols(branch_other, dense_other)).astype(bf16)
    attended, d_projected = attention(projected, d_mixed, tables, segment)

    def chunks_of(array, index):
        rows, columns = array.shape
        grouped = array.reshape(rows, columns // (2 * chunk), 2, chunk)
        return lax.dynamic_index_in_dim(grouped, index, 2, keepdims=False).reshape(rows, columns // 2)

    branch_pair = over_side(branch_half)

    def feature_sums(array):
        kept = chunks_of(array, side)
        got = over_side(chunks_of(array, 1 - side))
        own = in_order(col, kept, over_col(kept), 1)
        pair = in_order(col, got, over_col(got), 1)
        return (contract_rows(own, branch_half) + contract_rows(pair, branch_pair)).astype(bf16)

    def along_line(sums):
        depth = sums.shape[0] // line
        parts = sums.reshape(line, depth, sums.shape[1])

        def part(index):
            return lax.dynamic_index_in_dim(parts, jnp.clip(index, 0, line - 1), 0, keepdims=False).astype(f32)

        rightward, leftward = None, None
        for step in range(line - 1):
            right_part = part(line - 1 - step + place)
            left_part = part(place - (line - 1) + step)
            if step:
                right_part = right_part + rightward.astype(f32)
                left_part = left_part + leftward.astype(f32)
            to_right = [(2 * z + x, 2 * z + 2 + x) for z in range(min(step + 1, line - 1)) for x in range(2)]
            to_left = [(dp_size - 1 - p, dp_size - 1 - q) for p, q in to_right]
            rightward = lax.ppermute(right_part.astype(bf16), "dp", to_right)
            leftward = lax.ppermute(left_part.astype(bf16), "dp", to_left)
        return part(place) + rightward.astype(f32) + leftward.astype(f32)

    chunk = down_weight.shape[0] // dp_size
    grad_down = along_line(feature_sums(activated))

    chunk = up_weight.shape[0] // dp_size
    hidden_own = chunks_of(hidden, side)
    hidden_pair = over_side(chunks_of(hidden, 1 - side))

    def hidden_sums(array):
        pair = over_side(array)
        mine = (contract_rows(hidden_own, array) + contract_rows(hidden_pair, pair)).astype(bf16)
        theirs = (contract_rows(hidden_own, over_col(array)) + contract_rows(hidden_pair, over_col(pair))).astype(bf16)
        return in_order(col, along_line(mine), along_line(theirs), 1)

    grad_up = hidden_sums(d_before)
    chunk = dense_weight.shape[0] // dp_size
    grad_dense = along_line(feature_sums(attended))
    grad_qkv = hidden_sums(d_projected)

    def scatter(mine, other):
        half = mine + over_col(other.astype(bf16)).astype(f32)
        return half_at(half, row, 1) + over_row(half_at(half, 1 - row, 1).astype(bf16)).astype(f32)

    branch = scatter(
        dot_plain(attended, dense_mine) + dot_plain(activated, down_mine),
        dot_plain(attended, dense_other) + dot_plain(activated, down_other),
    )
    valid_col = is_valid.astype(f32)[:, None]
    outputs = (inputs.astype(f32) + valid_col * (branch + out_bias.astype(f32))).astype(bf16)

    d_hidden = scatter(
        contract_cols(d_projected, qkv_mine) + contract_cols(d_before, up_mine),
        contract_cols(d_projected, qkv_other) + contract_cols(d_before, up_other),
    )
    normed = (inputs.astype(f32) - average[:, None]) * scale_inv
    d_normed = d_hidden * norm_gain.astype(f32)
    row_sums = jnp.stack([jnp.sum(d_normed, axis=1), jnp.sum(d_normed * normed, axis=1)])
    row_sums = row_sums + over_row(row_sums)
    row_sums = row_sums + over_col(row_sums)
    grad_inputs = cotangent.astype(f32) + scale_inv * (
        d_normed - row_sums[0][:, None] / width - normed * row_sums[1][:, None] / width
    )

    small = [
        jnp.sum(d_hidden * normed, axis=0),
        jnp.sum(d_hidden, axis=0),
        jnp.sum(d_projected.astype(f32), axis=0),
        jnp.sum(d_before.astype(f32), axis=0),
        jnp.sum(grad_branch.astype(f32), axis=0),
    ]
    together = jnp.concatenate(small)
    bit = 1
    while bit < dp_size:
        together = together + lax.ppermute(together, "dp", [(e, e ^ bit) for e in range(dp_size)])
        bit *= 2
    ends = []
    for piece in small:
        ends.append((ends[-1] if ends else 0) + piece.shape[0])
    grad_gain, grad_shift, grad_qkv_bias, grad_up_bias, grad_out_bias = jnp.split(together, ends[:-1])
    return (
        outputs,
        grad_inputs,
        grad_gain,
        grad_shift,
        grad_qkv,
        grad_qkv_bias,
        grad_up,
        grad_up_bias,
        grad_dense,
        grad_down,
        grad_out_bias,
    )


def solution(mesh):
    in_specs = (
        P("dp", ("col", "row")),
        P(("col", "row")),
        P(("col", "row")),
        P("col", "row"),
        P(("row", "col")),
        P("col", "row"),
        P(("row", "col")),
        P("row", "col"),
        P("row", "col"),
        P(("col", "row")),
        P("dp", ("col", "row")),
        P(),
        P(),
    )
    out_specs = (
        P("dp", ("col", "row")),
        P("dp", ("col", "row")),
        P(("col", "row")),
        P(("col", "row")),
        P(("col", "dp"), "row"),
        P(("row", "col")),
        P(("col", "dp"), "row"),
        P(("row", "col")),
        P(("row", "dp"), "col"),
        P(("row", "dp"), "col"),
        P(("col", "row")),
    )
    return jax.shard_map(
        partial(on_device, mesh.shape["dp"]), mesh=mesh, in_specs=in_specs, out_specs=out_specs, check_vma=False
    )
```

time: 1160 us -> 526 us (0.45)
  the two profiles are of different devices: /device:TPU:9 before, /device:TPU:0 now
where the time goes in v1:
time: 526 us; the launch traced here: 516 us
  starting transfers between devices  173 us (33%)
  waiting for transfers between devices  122 us (23%)
  matrix products  107 us (20%)
  local copies, waits for them, and re-layouts  52 us (10%)
  Pallas kernels  31.3 us (6%)
  other arithmetic  27.9 us (5%)
    ppermute x18, starting transfers between devices, along_line(): rightward = lax.ppermute(right_part.astype(bf16), 'dp', to_right)  136 us
    ppermute x18, waiting for transfers between devices, along_line(): rightward = lax.ppermute(right_part.astype(bf16), 'dp', to_right)  84 us
    dot_general x8, matrix products, dot_plain(): return jnp.dot(left, right, preferred_element_type=f32)  38.5 us
    dot_general x8, matrix products, contract_cols(): lax.dot_general(left, right, (((1,), (1,)), ((), ())), preferred_element_...  35.1 us
    dot_general x12, matrix products, contract_rows(): lax.dot_general(left, right, (((0,), (0,)), ((), ())), preferred_element_...  33.2 us
    pallas_call x1, Pallas kernels, attention(): pl.pallas_call(attention_kernel, grid=(pairs,), in_specs=[pl.BlockSpec((r...  31.3 us
    unnamed x110, local copies, waits for them, and re-layouts  18.6 us
    ppermute x18, starting transfers between devices, along_line(): leftward = lax.ppermute(left_part.astype(bf16), 'dp', to_left)  17.4 us
  transfers between devices with their start and end apart: 69, of which 17 were waited for; matrix products, arithmetic and copies ran while one was open for 35% of the time, Pallas kernels for 6%

profile of v1, /device:TPU:0, one launch (start us, length us, event | category | flops | bytes accessed | tf_op | source)
XLA Modules:
  0.0 515.8 jit_solution(1744219840403550576)
XLA Ops:
  49.6 5.7 %fusion.15.proj_ref = f32[512,1536]{1,0:T(8,128)} fusion(f32[512,1536]{1,0:T(8,128)S(1)} %fusion.20, bf16[1024,1536]{1,0:T(8,128)(2,1)} %collective-permute-done.4, f32[1536]{0:T(1024)S(1)} %convert_element_type.522, bf16[512,1024]{0,1:T(8,128)(2,1)S(1)} %collective-permute-done.1, f32[1024]{0:T(1024)S(1)} %bitcast.242, f32[1024]{0:T(1024)S(1)} %bitcast.240, ...), kind=kOutput, calls=%fused_computation.26 | convolution fusion | flops 1615331328 | bytes 10504192 | tf_op jit(solution)/shard_map/dot_general | solution.py:137
  55.4 31.3 %attention.1 = (bf16[512,512]{1,0:T(8,128)(2,1)S(1)}, bf16[512,1536]{1,0:T(8,128)(2,1)}) custom-call(f32[512,1536]{1,0:T(8,128)} %fusion.15.proj_ref, bf16[512,512]{1,0:T(8,128)(2,1)S(1)} %fusion.46.mixed_ref, f32[3,512,64]{2,1,0:T(8,128)S(1)} %pad_maximum_fusion.4.tables_ref, s32[512,1]{1,0:T(8,128)S(1)} %copy-done.2, s32[1,512]{1,0:T(1,128)S(1)} %bitcast.194), custom_call_target="tpu_custom_call" | custom-call | flops 3758096384 | bytes 5505024 | tf_op jit(solution)/shard_map/attention/pallas_call | solution.py:108
  125.7 8.7 %multiply_convert_fusion = (bf16[512,2048]{1,0:T(8,128)(2,1)}, f32[512,2048]{1,0:T(8,128)}) fusion(f32[2048]{0:T(1024)S(1)} %convert_element_type.527, f32[512,2048]{1,0:T(8,128)S(1)} %copy-done.42, bf16[1024,2048]{1,0:T(8,128)(2,1)} %collective-permute-done.8, bf16[512,1024]{0,1:T(8,128)(2,1)S(1)} %copy-done.24, f32[1024]{0:T(1024)S(1)} %bitcast.243, ...), kind=kOutput, calls=%fused_computation.13 | convolution fusion | flops 2162163712 | bytes 15749120 | tf_op jit(solution)/shard_map/dot_general | solution.py:137
  137.7 6.5 %fusion.9 = f32[512,1024]{1,0:T(8,128)} fusion(bf16[512,2048]{1,0:T(8,128)(2,1)} %get-tuple-element.93, bf16[4096,1024]{1,0:T(8,128)(2,1)} %param.21, s32[]{:T(128)S(6)} %select_n.216), kind=kOutput, calls=%fused_computation.17 | convolution fusion | flops 2147483648 | bytes 8388612 | tf_op jit(solution)/shard_map/dot_general | solution.py:137
  154.3 8.0 %convert_reduce_fusion = (f32[2048]{0:T(1024)S(1)}, bf16[512,2048]{1,0:T(8,128)(2,1)S(1)}) fusion(f32[512,2048]{1,0:T(8,128)S(1)} %copy-done.43, f32[512,2048]{1,0:T(8,128)S(1)} %fusion.124, bf16[4096,1024]{1,0:T(8,128)(2,1)} %param.21, s32[]{:T(128)S(6)} %select_n.216, bf16[512,512]{0,1:T(8,128)(2,1)S(1)} %copy-done.18, bf16[512,512]{0,1:T(8,128)(2,1)S(1)} %copy-done.14), kind=kOutput, calls=%fused_computation.12 | convolution fusion | flops 2173696000 | bytes 15736836 | tf_op jit(solution)/shard_map/dot_general | solution.py:145
  170.9 5.9 %fusion.123 = f32[512,1024]{1,0:T(8,128)} fusion(bf16[512,2048]{1,0:T(8,128)(2,1)S(1)} %copy-done.31, bf16[2048,1024]{1,0:T(8,128)(2,1)} %collective-permute-done.9), kind=kOutput, calls=%fused_computation.245 | convolution fusion | flops 2147483648 | bytes 8388608 | tf_op jit(solution)/shard_map/dot_general | solution.py:137
  182.0 6.4 %constant_dynamic-slice_fusion.1 = (bf16[512,2,1,512]{3,2,1,0:T(2,128)(2,1)}, bf16[512,2,1,512]{3,2,1,0:T(2,128)(2,1)}) fusion(bf16[512,2,2,512]{3,2,1,0:T(2,128)(2,1)S(1)} %reshape.231, s32[]{:T(128)S(6)} %select_n.222, s32[]{:T(128)S(6)} %select_n.223), kind=kLoop, calls=%fused_computation.200 | loop fusion | bytes 4194312 | tf_op jit(solution)/shard_map/jit(dynamic_index_in_dim)/dynamic_slice | solution.py:228
  192.0 6.0 %copy.54 = bf16[512,2,1,512]{0,3,1,2:T(8,128)(2,1)} copy(bf16[512,2,1,512]{3,2,1,0:T(2,128)(2,1)} %get-tuple-element.39) | data formatting | bytes 2097152
  209.2 8.1 %collective-permute-start.56 = (bf16[128,1024]{1,0:T(8,128)(2,1)S(1)}, bf16[128,1024]{1,0:T(8,128)(2,1)S(1)}, u32[]{:S(2)}, u32[]{:S(2)}) collective-permute-start(bf16[128,1024]{1,0:T(8,128)(2,1)S(1)} %get-tuple-element.58), channel_id=1, source_target_pairs={{0,8},{4,12},{8,16},{12,20},{16,24},{20,28},{1,9},{5,13},{9,17},{1... | collective-permute-start | bytes 786440 | tf_op jit(solution)/shard_map/ppermute | solution.py:255
  243.4 6.3 %collective-permute-done.22 = bf16[128,1536]{1,0:T(8,128)(2,1)S(1)} collective-permute-done((bf16[128,1536]{1,0:T(8,128)(2,1)S(1)}, bf16[128,1536]{1,0:T(8,128)(2,1)S(1)}, u32[]{:S(2)}, u32[]{:S(2)}) %collective-permute-start.22) | collective-permute-done | bytes 393248 | tf_op jit(solution)/shard_map/ppermute | solution.py:255
  250.4 5.9 %collective-permute-done.13 = bf16[512,512]{1,0:T(8,128)(2,1)S(1)} collective-permute-done((bf16[512,512]{1,0:T(8,128)(2,1)S(1)}, bf16[512,512]{1,0:T(8,128)(2,1)S(1)}, u32[]{:S(2)}, u32[]{:S(2)}) %collective-permute-start.13) | collective-permute-done | bytes 524320 | tf_op jit(solution)/shard_map/ppermute | solution.py:279
  257.6 9.4 %collective-permute-done.14 = f32[2,512]{1,0:T(2,128)S(1)} collective-permute-done((f32[2,512]{1,0:T(2,128)S(1)}, f32[2,512]{1,0:T(2,128)S(1)}, u32[]{:S(2)}, u32[]{:S(2)}) %collective-permute-start.14) | collective-permute-done | bytes 4128 | tf_op jit(solution)/shard_map/ppermute | solution.py:295
  282.2 6.5 %collective-permute-done.18 = f32[5120]{0:T(1024)S(1)} collective-permute-done((f32[5120]{0:T(1024)S(1)}, f32[5120]{0:T(1024)S(1)}, u32[]{:S(2)}, u32[]{:S(2)}) %collective-permute-start.18) | collective-permute-done | bytes 20512 | tf_op jit(solution)/shard_map/ppermute | solution.py:311
  301.0 7.2 %fusion.37 = f32[2048,1024]{1,0:T(8,128)} fusion(bf16[512,1024]{0,1:T(8,128)(2,1)} %collective-permute-done.53, bf16[512,1024]{0,1:T(8,128)(2,1)S(1)} %get-tuple-element.41, bf16[512,1024]{0,1:T(8,128)(2,1)S(1)} %get-tuple-element.40), kind=kOutput, calls=%fused_computation.54 | convolution fusion | flops 2151677952 | bytes 11534336 | tf_op jit(solution)/shard_map/dot_general | solution.py:141
  308.2 5.8 %add_convert_fusion = bf16[2048,1024]{1,0:T(8,128)(2,1)S(1)} fusion(f32[2048,1024]{1,0:T(8,128)} %fusion.37, bf16[512,1024]{0,1:T(8,128)(2,1)S(1)} %get-tuple-element.37, bf16[512,1024]{0,1:T(8,128)(2,1)S(1)} %get-tuple-element.36, bf16[512,512]{0,1:T(8,128)(2,1)S(1)} %copy-done.19, bf16[512,512]{0,1:T(8,128)(2,1)S(1)} %copy-done.15), kind=kOutput, calls=%fused_computation | convolution fusion | flops 2157969408 | bytes 15728640 | tf_op jit(solution)/shard_map/dot_general | solution.py:141
  314.2 6.6 %collective-permute-done.29 = bf16[128,1536]{1,0:T(8,128)(2,1)S(1)} collective-permute-done((bf16[128,1536]{1,0:T(8,128)(2,1)S(1)}, bf16[128,1536]{1,0:T(8,128)(2,1)S(1)}, u32[]{:S(2)}, u32[]{:S(2)}) %collective-permute-start.29) | collective-permute-done | bytes 393248 | tf_op jit(solution)/shard_map/ppermute | solution.py:255
  327.5 28.6 %collective-permute-done.30 = bf16[128,1536]{1,0:T(8,128)(2,1)S(1)} collective-permute-done((bf16[128,1536]{1,0:T(8,128)(2,1)S(1)}, bf16[128,1536]{1,0:T(8,128)(2,1)S(1)}, u32[]{:S(2)}, u32[]{:S(2)}) %collective-permute-start.30) | collective-permute-done | bytes 393248 | tf_op jit(solution)/shard_map/ppermute | solution.py:255
  363.2 7.7 %collective-permute-done.37 = bf16[128,2048]{1,0:T(8,128)(2,1)S(1)} collective-permute-done((bf16[128,2048]{1,0:T(8,128)(2,1)S(1)}, bf16[128,2048]{1,0:T(8,128)(2,1)S(1)}, u32[]{:S(2)}, u32[]{:S(2)}) %collective-permute-start.37) | collective-permute-done | bytes 524320 | tf_op jit(solution)/shard_map/ppermute | solution.py:255
  378.5 17.4 %collective-permute-done.64 = bf16[512,1024]{1,0:T(8,128)(2,1)S(1)} collective-permute-done((bf16[512,1024]{1,0:T(8,128)(2,1)S(1)}, bf16[512,1024]{1,0:T(8,128)(2,1)S(1)}, u32[]{:S(2)}, u32[]{:S(2)}) %collective-permute-start.64) | collective-permute-done | bytes 1048608 | tf_op jit(solution)/shard_map/ppermute | solution.py:255
  402.2 6.7 %collective-permute-done.44 = bf16[128,2048]{1,0:T(8,128)(2,1)S(1)} collective-permute-done((bf16[128,2048]{1,0:T(8,128)(2,1)S(1)}, bf16[128,2048]{1,0:T(8,128)(2,1)S(1)}, u32[]{:S(2)}, u32[]{:S(2)}) %collective-permute-start.44) | collective-permute-done | bytes 524320 | tf_op jit(solution)/shard_map/ppermute | solution.py:255
  414.3 12.7 %collective-permute-start.31 = (bf16[128,1536]{1,0:T(8,128)(2,1)S(1)}, bf16[128,1536]{1,0:T(8,128)(2,1)S(1)}, u32[]{:S(2)}, u32[]{:S(2)}) collective-permute-start(bf16[128,1536]{1,0:T(8,128)(2,1)S(1)} %get-tuple-element.50), channel_id=1, source_target_pairs={{0,8},{4,12},{8,16},{12,20},{16,24},{20,28},{1,9},{5,13},{9,17},{1... | collective-permute-start | bytes 1179656 | tf_op jit(solution)/shard_map/ppermute | solution.py:255
  428.8 12.6 %collective-permute-start.65 = (bf16[512,1024]{1,0:T(8,128)(2,1)S(1)}, bf16[512,1024]{1,0:T(8,128)(2,1)S(1)}, u32[]{:S(2)}, u32[]{:S(2)}) collective-permute-start(bf16[512,1024]{1,0:T(8,128)(2,1)S(1)} %get-tuple-element.32), channel_id=1, source_target_pairs={{0,8},{4,12},{8,16},{12,20},{16,24},{20,28},{1,9},{5,13},{9,17},{1... | collective-permute-start | bytes 3145736 | tf_op jit(solution)/shard_map/ppermute | solution.py:255
  441.8 8.5 %collective-permute-start.38 = (bf16[128,2048]{1,0:T(8,128)(2,1)S(1)}, bf16[128,2048]{1,0:T(8,128)(2,1)S(1)}, u32[]{:S(2)}, u32[]{:S(2)}) collective-permute-start(bf16[128,2048]{1,0:T(8,128)(2,1)S(1)} %get-tuple-element.46), channel_id=1, source_target_pairs={{0,8},{4,12},{8,16},{12,20},{16,24},{20,28},{1,9},{5,13},{9,17},{1... | collective-permute-start | bytes 1572872 | tf_op jit(solution)/shard_map/ppermute | solution.py:255
  454.1 46.7 %collective-permute-start.46 = (bf16[128,2048]{1,0:T(8,128)(2,1)S(1)}, bf16[128,2048]{1,0:T(8,128)(2,1)S(1)}, u32[]{:S(2)}, u32[]{:S(2)}) collective-permute-start(bf16[128,2048]{1,0:T(8,128)(2,1)S(1)} %get-tuple-element.42), channel_id=1, source_target_pairs={{0,8},{4,12},{8,16},{12,20},{16,24},{20,28},{1,9},{5,13},{9,17},{1... | collective-permute-start | bytes 1572872 | tf_op jit(solution)/shard_map/ppermute | solution.py:255
  (360 shorter events, 237.8 us)
Async XLA Ops:
  15.9 33.7 %collective-permute-start.4 = (bf16[1024,1536]{1,0:T(8,128)(2,1)}, bf16[1024,1536]{1,0:T(8,128)(2,1)}, u32[]{:S(2)}, u32[]{:S(2)}) collective-permute-start(bf16[1024,1536]{1,0:T(8,128)(2,1)} %constant_dynamic-slice_fusion.9), channel_id=1, source_target_pairs={{0,1},{1,0},{2,3},{3,2},{4,5},{5,4},{6,7},{7,6},{8,9},{9,8},{10,11... | collective-permute-start | bytes 9437192 | tf_op jit(solution)/shard_map/ppermute | solution.py:199
  35.1 88.8 %collective-permute-start.8 = (bf16[1024,2048]{1,0:T(8,128)(2,1)}, bf16[1024,2048]{1,0:T(8,128)(2,1)}, u32[]{:S(2)}, u32[]{:S(2)}) collective-permute-start(bf16[1024,2048]{1,0:T(8,128)(2,1)} %constant_dynamic-slice_fusion.7), channel_id=1, source_target_pairs={{0,1},{1,0},{2,3},{3,2},{4,5},{5,4},{6,7},{7,6},{8,9},{9,8},{10,11... | collective-permute-start | bytes 12582920 | tf_op jit(solution)/shard_map/ppermute | solution.py:197
  36.0 108.2 %collective-permute-start.9 = (bf16[2048,1024]{1,0:T(8,128)(2,1)}, bf16[2048,1024]{1,0:T(8,128)(2,1)}, u32[]{:S(2)}, u32[]{:S(2)}) collective-permute-start(bf16[2048,1024]{1,0:T(8,128)(2,1)} %constant_dynamic-slice_fusion.6), channel_id=1, source_target_pairs={{0,1},{1,0},{2,3},{3,2},{4,5},{5,4},{6,7},{7,6},{8,9},{9,8},{10,11... | collective-permute-start | bytes 12582920 | tf_op jit(solution)/shard_map/ppermute | solution.py:198
  36.9 73.9 %collective-permute-start.53 = (bf16[512,1024]{0,1:T(8,128)(2,1)}, bf16[512,1024]{0,1:T(8,128)(2,1)}, u32[]{:S(2)}, u32[]{:S(2)}) collective-permute-start(bf16[512,1024]{0,1:T(8,128)(2,1)} %pad_maximum_fusion.3), channel_id=1, source_target_pairs={{0,4},{4,0},{8,12},{12,8},{16,20},{20,16},{24,28},{28,24},{1,5},{5... | collective-permute-start | bytes 3145736 | tf_op jit(solution)/shard_map/ppermute | solution.py:230
  107.6 101.6 %collective-permute-start.19 = (bf16[512,512]{0,1:T(8,128)(2,1)}, bf16[512,512]{0,1:T(8,128)(2,1)S(1)}, u32[]{:S(2)}, u32[]{:S(2)}) collective-permute-start(bf16[512,512]{0,1:T(8,128)(2,1)} %bitcast.20), channel_id=1, source_target_pairs={{0,4},{4,0},{8,12},{12,8},{16,20},{20,16},{24,28},{28,24},{1,5},{5... | collective-permute-start | bytes 1572872 | tf_op jit(solution)/shard_map/ppermute | solution.py:264
  109.0 108.3 %collective-permute-start.20 = (bf16[512,1536]{1,0:T(8,128)(2,1)}, bf16[512,1536]{1,0:T(8,128)(2,1)}, u32[]{:S(2)}, u32[]{:S(2)}) collective-permute-start(bf16[512,1536]{1,0:T(8,128)(2,1)} %get-tuple-element.14), channel_id=1, source_target_pairs={{0,4},{4,0},{8,12},{12,8},{16,20},{20,16},{24,28},{28,24},{1,5},{5... | collective-permute-start | bytes 4718600 | tf_op jit(solution)/shard_map/ppermute | solution.py:267
  123.1 98.0 %collective-permute-start.27 = (bf16[512,1536]{1,0:T(8,128)(2,1)}, bf16[512,1536]{1,0:T(8,128)(2,1)}, u32[]{:S(2)}, u32[]{:S(2)}) collective-permute-start(bf16[512,1536]{1,0:T(8,128)(2,1)} %get-tuple-element.14), channel_id=1, source_target_pairs={{0,1},{1,0},{2,3},{3,2},{4,5},{5,4},{6,7},{7,6},{8,9},{9,8},{10,11... | collective-permute-start | bytes 4718600 | tf_op jit(solution)/shard_map/ppermute | solution.py:269
  123.9 78.4 %collective-permute-start.57 = (bf16[128,1024]{1,0:T(8,128)(2,1)S(1)}, bf16[128,1024]{1,0:T(8,128)(2,1)}, u32[]{:S(2)}, u32[]{:S(2)}) collective-permute-start(bf16[128,1024]{1,0:T(8,128)(2,1)S(1)} %get-tuple-element.61), channel_id=1, source_target_pairs={{28,20},{24,16},{29,21},{25,17},{30,22},{26,18},{31,23},{27,19}} | collective-permute-start | bytes 786440 | tf_op jit(solution)/shard_map/ppermute | solution.py:256
  144.2 59.4 %collective-permute-start.55 = (bf16[128,1024]{1,0:T(8,128)(2,1)}, bf16[128,1024]{1,0:T(8,128)(2,1)}, u32[]{:S(2)}, u32[]{:S(2)}) collective-permute-start(bf16[128,1024]{1,0:T(8,128)(2,1)} %fusion.92), channel_id=1, source_target_pairs={{0,8},{4,12},{8,16},{12,20},{1,9},{5,13},{9,17},{13,21},{2,10},{6,... | collective-permute-start | bytes 786440 | tf_op jit(solution)/shard_map/ppermute | solution.py:255
  202.3 89.7 %collective-permute-start.35 = (bf16[512,2048]{1,0:T(8,128)(2,1)}, bf16[512,2048]{1,0:T(8,128)(2,1)S(1)}, u32[]{:S(2)}, u32[]{:S(2)}) collective-permute-start(bf16[512,2048]{1,0:T(8,128)(2,1)} %copy-done.29), channel_id=1, source_target_pairs={{0,4},{4,0},{8,12},{12,8},{16,20},{20,16},{24,28},{28,24},{1,5},{5... | collective-permute-start | bytes 6291464 | tf_op jit(solution)/shard_map/ppermute | solution.py:267
  228.6 67.5 %collective-permute-start.42 = (bf16[512,2048]{1,0:T(8,128)(2,1)S(1)}, bf16[512,2048]{1,0:T(8,128)(2,1)S(1)}, u32[]{:S(2)}, u32[]{:S(2)}) collective-permute-start(bf16[512,2048]{1,0:T(8,128)(2,1)S(1)} %copy-done.30), channel_id=1, source_target_pairs={{0,1},{1,0},{2,3},{3,2},{4,5},{5,4},{6,7},{7,6},{8,9},{9,8},{10,11... | collective-permute-start | bytes 6291464 | tf_op jit(solution)/shard_map/ppermute | solution.py:269
  242.7 39.5 %collective-permute-start.61 = (bf16[512,1024]{0,1:T(8,128)(2,1)S(1)}, bf16[512,1024]{0,1:T(8,128)(2,1)S(1)}, u32[]{:S(2)}, u32[]{:S(2)}) collective-permute-start(bf16[512,1024]{0,1:T(8,128)(2,1)S(1)} %bitcast.238), channel_id=1, source_target_pairs={{0,4},{4,0},{8,12},{12,8},{16,20},{20,16},{24,28},{28,24},{1,5},{5... | collective-permute-start | bytes 3145736 | tf_op jit(solution)/shard_map/ppermute | solution.py:234
  290.5 151.3 %collective-permute-start.23 = (bf16[128,1536]{1,0:T(8,128)(2,1)S(1)}, bf16[128,1536]{1,0:T(8,128)(2,1)S(1)}, u32[]{:S(2)}, u32[]{:S(2)}) collective-permute-start(bf16[128,1536]{1,0:T(8,128)(2,1)S(1)} %get-tuple-element.54), channel_id=1, source_target_pairs={{0,8},{4,12},{8,16},{12,20},{16,24},{20,28},{1,9},{5,13},{9,17},{1... | collective-permute-start | bytes 1179656 | tf_op jit(solution)/shard_map/ppermute | solution.py:255
  293.4 31.9 %collective-permute-start.36 = (bf16[128,2048]{1,0:T(8,128)(2,1)S(1)}, bf16[128,2048]{1,0:T(8,128)(2,1)S(1)}, u32[]{:S(2)}, u32[]{:S(2)}) collective-permute-start(bf16[128,2048]{1,0:T(8,128)(2,1)S(1)} %get-tuple-element.48), channel_id=1, source_target_pairs={{0,8},{4,12},{1,9},{5,13},{2,10},{6,14},{3,11},{7,15}} | collective-permute-start | bytes 1572872 | tf_op jit(solution)/shard_map/ppermute | solution.py:255
  296.1 79.7 %collective-permute-start.43 = (bf16[512,2048]{1,0:T(8,128)(2,1)S(1)}, bf16[512,2048]{1,0:T(8,128)(2,1)S(1)}, u32[]{:S(2)}, u32[]{:S(2)}) collective-permute-start(bf16[512,2048]{1,0:T(8,128)(2,1)S(1)} %collective-permute-done.35), channel_id=1, source_target_pairs={{0,1},{1,0},{2,3},{3,2},{4,5},{5,4},{6,7},{7,6},{8,9},{9,8},{10,11... | collective-permute-start | bytes 6291464 | tf_op jit(solution)/shard_map/ppermute | solution.py:269
  320.8 39.9 %collective-permute-start.63 = (bf16[512,1024]{1,0:T(8,128)(2,1)S(1)}, bf16[512,1024]{1,0:T(8,128)(2,1)S(1)}, u32[]{:S(2)}, u32[]{:S(2)}) collective-permute-start(bf16[512,1024]{1,0:T(8,128)(2,1)S(1)} %get-tuple-element.34), channel_id=1, source_target_pairs={{0,8},{4,12},{1,9},{5,13},{2,10},{6,14},{3,11},{7,15}} | collective-permute-start | bytes 3145736 | tf_op jit(solution)/shard_map/ppermute | solution.py:255
  326.8 35.6 %collective-permute-start.39 = (bf16[128,2048]{1,0:T(8,128)(2,1)S(1)}, bf16[128,2048]{1,0:T(8,128)(2,1)S(1)}, u32[]{:S(2)}, u32[]{:S(2)}) collective-permute-start(bf16[128,2048]{1,0:T(8,128)(2,1)S(1)} %get-tuple-element.49), channel_id=1, source_target_pairs={{28,20},{24,16},{29,21},{25,17},{30,22},{26,18},{31,23},{27,19}} | collective-permute-start | bytes 1572872 | tf_op jit(solution)/shard_map/ppermute | solution.py:256
  360.7 89.7 %collective-permute-start.26 = (bf16[128,1536]{1,0:T(8,128)(2,1)S(1)}, bf16[128,1536]{1,0:T(8,128)(2,1)S(1)}, u32[]{:S(2)}, u32[]{:S(2)}) collective-permute-start(bf16[128,1536]{1,0:T(8,128)(2,1)S(1)} %fusion.77), channel_id=1, source_target_pairs={{28,20},{24,16},{20,12},{16,8},{12,4},{8,0},{29,21},{25,17},{21,13... | collective-permute-start | bytes 1179656 | tf_op jit(solution)/shard_map/ppermute | solution.py:256
  414.3 37.4 %collective-permute-start.31 = (bf16[128,1536]{1,0:T(8,128)(2,1)S(1)}, bf16[128,1536]{1,0:T(8,128)(2,1)S(1)}, u32[]{:S(2)}, u32[]{:S(2)}) collective-permute-start(bf16[128,1536]{1,0:T(8,128)(2,1)S(1)} %get-tuple-element.50), channel_id=1, source_target_pairs={{0,8},{4,12},{8,16},{12,20},{16,24},{20,28},{1,9},{5,13},{9,17},{1... | collective-permute-start | bytes 1179656 | tf_op jit(solution)/shard_map/ppermute | solution.py:255
  428.8 72.1 %collective-permute-start.65 = (bf16[512,1024]{1,0:T(8,128)(2,1)S(1)}, bf16[512,1024]{1,0:T(8,128)(2,1)S(1)}, u32[]{:S(2)}, u32[]{:S(2)}) collective-permute-start(bf16[512,1024]{1,0:T(8,128)(2,1)S(1)} %get-tuple-element.32), channel_id=1, source_target_pairs={{0,8},{4,12},{8,16},{12,20},{16,24},{20,28},{1,9},{5,13},{9,17},{1... | collective-permute-start | bytes 3145736 | tf_op jit(solution)/shard_map/ppermute | solution.py:255
  441.8 63.5 %collective-permute-start.38 = (bf16[128,2048]{1,0:T(8,128)(2,1)S(1)}, bf16[128,2048]{1,0:T(8,128)(2,1)S(1)}, u32[]{:S(2)}, u32[]{:S(2)}) collective-permute-start(bf16[128,2048]{1,0:T(8,128)(2,1)S(1)} %get-tuple-element.46), channel_id=1, source_target_pairs={{0,8},{4,12},{8,16},{12,20},{16,24},{20,28},{1,9},{5,13},{9,17},{1... | collective-permute-start | bytes 1572872 | tf_op jit(solution)/shard_map/ppermute | solution.py:255
  450.4 55.0 %collective-permute-start.41 = (bf16[128,2048]{1,0:T(8,128)(2,1)S(1)}, bf16[128,2048]{1,0:T(8,128)(2,1)S(1)}, u32[]{:S(2)}, u32[]{:S(2)}) collective-permute-start(bf16[128,2048]{1,0:T(8,128)(2,1)S(1)} %fusion.64), channel_id=1, source_target_pairs={{28,20},{24,16},{20,12},{16,8},{12,4},{8,0},{29,21},{25,17},{21,13... | collective-permute-start | bytes 1572872 | tf_op jit(solution)/shard_map/ppermute | solution.py:256
  451.7 51.8 %collective-permute-start.68 = (bf16[512,1024]{1,0:T(8,128)(2,1)S(1)}, bf16[512,1024]{1,0:T(8,128)(2,1)S(1)}, u32[]{:S(2)}, u32[]{:S(2)}) collective-permute-start(bf16[512,1024]{1,0:T(8,128)(2,1)S(1)} %fusion.42), channel_id=1, source_target_pairs={{28,20},{24,16},{20,12},{16,8},{12,4},{8,0},{29,21},{25,17},{21,13... | collective-permute-start | bytes 3145736 | tf_op jit(solution)/shard_map/ppermute | solution.py:256
  454.1 54.1 %collective-permute-start.46 = (bf16[128,2048]{1,0:T(8,128)(2,1)S(1)}, bf16[128,2048]{1,0:T(8,128)(2,1)S(1)}, u32[]{:S(2)}, u32[]{:S(2)}) collective-permute-start(bf16[128,2048]{1,0:T(8,128)(2,1)S(1)} %get-tuple-element.42), channel_id=1, source_target_pairs={{0,8},{4,12},{8,16},{12,20},{16,24},{20,28},{1,9},{5,13},{9,17},{1... | collective-permute-start | bytes 1572872 | tf_op jit(solution)/shard_map/ppermute | solution.py:255
  (95 other events, 1087.8 us)
